TPU v7x, 128 devices: a whole 4x4x4 slice. The times are simulated.
128 devices in a mesh: ctx: 32 (over y, x, core), head: 4 (over z).
Axes of the slice: x: 4, y: 4, z: 4, core: 2. Of those that a mesh axis runs over, the one named last changes fastest.
Arguments:
- queries: bfloat16 [16384, 4096], P('ctx', 'head'), may hold values from -5 to 5
- keys: bfloat16 [16384, 512], P('ctx', 'head'), may hold values from -5 to 5
- values: bfloat16 [16384, 512], P('ctx', 'head'), may hold values from -6 to 6
- doc_ids: int32 [16384], replicated, may hold values from 0 to 31, never falling along the last dimension, each value on 1 to 1536 neighbouring positions
- out_weight: bfloat16 [4096, 8192], P(None, 'head'), may hold values from -0.09375 to 0.09375
Outputs:
- layer_out: bfloat16 [16384, 8192], P('ctx', 'head')
Inputs may be any that keep to these rules, and one draw needn't show every extreme that they name: `doc_ids`: every document holds at most 1536 tokens, and one holds exactly that many.
All inputs are finite; a program needn't handle non-finite values.
Results may differ from a plain program's by a relative error of at most 0.0053.
Values may be sent and summed in bfloat16 or wider, within the bound.
No kernel may reach another device: no remote copies, remote signals or barrier semaphores. Data moves between devices by JAX's collectives and lax.ppermute only.
A program may use at most 128 MiB of HBM per device.

v0:
```python
import functools
import math

import jax
import jax.numpy as jnp
from jax import lax
from jax.experimental import pallas as pl
from jax.experimental.pallas import tpu as pltpu
from jax.sharding import PartitionSpec as P

HEAD_SIZE = 128
REACH = 3
EXPONENT_SCALE = math.log2(math.e) * HEAD_SIZE ** (-0.5)
HIDDEN = -1e30
CONTRACT_LAST = (((1,), (1,)), ((), ()))
PLAIN = (((1,), (0,)), ((), ()))
VMEM = pl.BlockSpec(memory_space=pltpu.VMEM)
SMEM = pl.BlockSpec(memory_space=pltpu.SMEM)


def beside_ones(values):
    return jnp.concatenate([values, jnp.ones_like(values)], 1)


def wide(column, count):
    return column if count == 1 else jnp.concatenate([column] * count, 1)


def block_update(q, keys, values, bias, before, mixed):
    span = keys.shape[0]
    s = lax.dot_general(q, keys, CONTRACT_LAST, preferred_element_type=jnp.float32)
    if bias is not None:
        s = s + bias
    peak = jnp.broadcast_to(jnp.max(s, axis=1, keepdims=True), (q.shape[0], HEAD_SIZE))
    if before is not None:
        peak = jnp.maximum(before, peak)
    weights = jnp.exp2((s - wide(peak, span // HEAD_SIZE)) * EXPONENT_SCALE).astype(jnp.bfloat16)
    mix = lax.dot_general(weights, beside_ones(values), PLAIN, preferred_element_type=jnp.float32)
    if before is not None:
        mix = mix + mixed * wide(jnp.exp2((before - peak) * EXPONENT_SCALE), 2)
    return peak, mix


def own_kernel(splits, q_ref, own_ref, kdoc_ref, *refs):
    *states, qdoc_ref, again_ref, bias_ref = refs
    again_ref[...] = own_ref[...]
    rows = q_ref.shape[0]
    half = rows // 2
    heads = q_ref.shape[1] // HEAD_SIZE
    own_at = REACH * rows
    qdoc_ref[...] = jnp.broadcast_to(kdoc_ref[0:1, own_at:own_at + rows], (HEAD_SIZE, rows)).T
    for part in range(2):
        span = (part + 1) * half
        at = part * half
        row = at + lax.broadcasted_iota(jnp.int32, (half, span), 0)
        col = lax.broadcasted_iota(jnp.int32, (half, span), 1)
        doc = wide(qdoc_ref[at:at + half, :], span // HEAD_SIZE)
        seen = (doc == kdoc_ref[0:1, own_at:own_at + span]) & (col <= row)
        bias_ref[:, 0:span] = jnp.where(seen, 0.0, HIDDEN)
        for head in range(heads):
            q = q_ref[at:at + half, head * HEAD_SIZE:(head + 1) * HEAD_SIZE]
            peak, mix = block_update(q, own_ref[0:span, :], own_ref[rows:rows + span, :], bias_ref[:, 0:span], None, None)
            group = sum(head >= first for first in splits) - 1
            states[2 * group][head - splits[group], at:at + half, :] = peak
            states[2 * group + 1][head - splits[group], at:at + half, :] = mix


def update_seen(docs_ref, q_ref, qdoc_ref, kdoc_ref, bias_ref, blocks, states):
    rows = q_ref.shape[0]
    half = rows // 2

    own_at = REACH * rows

    def update(row_at, ref, shard, at, span, masked):
        here = pl.ds(row_at, half)
        keys = ref[pl.ds(at, span), :]
        values = ref[pl.ds(rows + at, span), :]
        if masked:
            doc = wide(qdoc_ref[here, :], span // HEAD_SIZE)
            window_at = pl.ds(pl.multiple_of(shard * rows + at, HEAD_SIZE), span)
            bias_ref[:, 0:span] = jnp.where(doc == kdoc_ref[0:1, window_at], 0.0, HIDDEN)
        for first_head, peak_ref, mix_ref in states:
            for head in range(peak_ref.shape[0]):
                column = (first_head + head) * HEAD_SIZE
                peak, mix = block_update(
                    q_ref[here, column:column + HEAD_SIZE], keys, values,
                    bias_ref[:, 0:span] if masked else None, peak_ref[head, here, :], mix_ref[head, here, :])
                peak_ref[head, here, :] = peak
                mix_ref[head, here, :] = mix

    @pl.loop(0, rows // half)
    def _(part):
        row_at = pl.multiple_of(part * half, half)
        first_doc = docs_ref[own_at + row_at]
        last_doc = docs_ref[own_at + row_at + half - 1]
        for ref, shard, span in blocks:
            @pl.loop(0, rows // span)
            def _(piece):
                at = pl.multiple_of(piece * span, span)
                lo, hi = docs_ref[shard * rows + at], docs_ref[shard * rows + at + span - 1]

                @pl.when((hi == first_doc) & (lo == last_doc))
                def _():
                    update(row_at, ref, shard, at, span, False)

                @pl.when((hi == first_doc) & (lo != last_doc))
                def _():
                    update(row_at, ref, shard, at, span, True)


def two_behind_kernel(docs_ref, q_ref, k2_ref, qdoc_ref, kdoc_ref, _, __, peak_ref, mix_ref, bias_ref):
    blocks = ((k2_ref, 1, q_ref.shape[0]),)
    update_seen(docs_ref, q_ref, qdoc_ref, kdoc_ref, bias_ref, blocks, ((0, peak_ref, mix_ref),))


def rest_kernel(first_head, heads, fetches, all_blocks, docs_ref, q_ref, beside_ref, k2_ref, beside_two_ref, three_ref,
                qdoc_ref, kdoc_ref, *refs):
    if fetches:
        weight_ref, _, _, peak_ref, mix_ref, out_ref, held_ref, bias_ref, k1_ref, k3_ref, fetched = refs
        fetch = pltpu.make_async_copy(weight_ref, held_ref, fetched)
        fetch.start()
    else:
        _, _, peak_ref, mix_ref, out_ref, bias_ref, k1_ref, k3_ref = refs
    rows = q_ref.shape[0]
    half = rows // 2
    second_core = lax.rem(lax.axis_index("ctx"), 2) == 1

    @pl.when(second_core)
    def _():
        k1_ref[...] = beside_ref[...]
        k3_ref[...] = beside_two_ref[...]

    @pl.when(jnp.logical_not(second_core))
    def _():
        k1_ref[...] = beside_two_ref[...]
        k3_ref[...] = three_ref[...]

    blocks = ((k1_ref, 2, rows), (k3_ref, 0, half))
    if all_blocks:
        blocks += ((k2_ref, 1, rows),)
    update_seen(docs_ref, q_ref, qdoc_ref, kdoc_ref, bias_ref, blocks, ((first_head, peak_ref, mix_ref),))
    for head in range(heads):
        mix = mix_ref[head, :, 0:HEAD_SIZE] / mix_ref[head, :, HEAD_SIZE:]
        out_ref[:, head * HEAD_SIZE:(head + 1) * HEAD_SIZE] = mix.astype(jnp.bfloat16)
    if fetches:
        fetch.wait()


def state_shapes(heads, rows):
    return [
        jax.ShapeDtypeStruct((heads, rows, HEAD_SIZE), jnp.float32),
        jax.ShapeDtypeStruct((heads, rows, 2 * HEAD_SIZE), jnp.float32),
    ]


ATTEND_COST = pl.CostEstimate(flops=2**32, bytes_accessed=2**20, transcendentals=2**20)


def attend_own(queries, own, kdoc, splits):
    rows, width = queries.shape
    ends = splits[1:] + (width // HEAD_SIZE,)
    return pl.pallas_call(
        functools.partial(own_kernel, splits),
        in_specs=[VMEM] * 3,
        out_specs=[VMEM] * (2 * len(splits) + 2),
        scratch_shapes=[pltpu.VMEM((rows // 2, rows), jnp.float32)],
        out_shape=[shape for first, end in zip(splits, ends) for shape in state_shapes(end - first, rows)]
        + [jax.ShapeDtypeStruct((rows, HEAD_SIZE), jnp.int32), jax.ShapeDtypeStruct(own.shape, own.dtype)],
        compiler_params=pltpu.CompilerParams(vmem_limit_bytes=8 * 2**20),
        cost_estimate=ATTEND_COST,
        name="attend_own",
    )(queries, own, kdoc)


def attend_two_behind(queries, block, qdoc, kdoc, state):
    rows = queries.shape[0]
    return pl.pallas_call(
        two_behind_kernel,
        in_specs=[SMEM] + [VMEM] * 6,
        out_specs=[VMEM] * 2,
        scratch_shapes=[pltpu.VMEM((rows // 2, rows), jnp.float32)],
        out_shape=state_shapes(state[0].shape[0], rows),
        input_output_aliases={5: 0, 6: 1},
        compiler_params=pltpu.CompilerParams(vmem_limit_bytes=8 * 2**20),
        cost_estimate=ATTEND_COST,
        name="attend_two_behind",
    )(kdoc.reshape(-1), queries, block, qdoc, kdoc, *state)


def attend_rest(queries, parts, qdoc, kdoc, state, first_head, all_blocks, weight=None):
    rows = queries.shape[0]
    heads = state[0].shape[0]
    fetches = weight is not None
    attended = jax.ShapeDtypeStruct((rows, heads * HEAD_SIZE), jnp.bfloat16)
    return pl.pallas_call(
        functools.partial(rest_kernel, first_head, heads, fetches, all_blocks),
        in_specs=[SMEM] + [VMEM] * 7 + [pl.BlockSpec(memory_space=pl.ANY)] * fetches + [VMEM] * 2,
        out_specs=[VMEM] * (3 + fetches),
        scratch_shapes=[
            pltpu.VMEM((rows // 2, rows), jnp.float32),
            pltpu.VMEM(parts[0].shape, jnp.bfloat16),
            pltpu.VMEM(parts[0].shape, jnp.bfloat16),
        ] + [pltpu.SemaphoreType.DMA] * fetches,
        out_shape=state_shapes(heads, rows) + [attended]
        + ([jax.ShapeDtypeStruct(weight.shape, weight.dtype)] if fetches else []),
        input_output_aliases={8 + fetches: 0, 9 + fetches: 1},
        compiler_params=pltpu.CompilerParams(vmem_limit_bytes=(24 if fetches else 8) * 2**20),
        cost_estimate=ATTEND_COST,
        name=f"attend_rest_{first_head}",
    )(kdoc.reshape(-1), queries, *parts, qdoc, kdoc, *[weight] * fetches, *state)[2:]


def project_kernel(count, carried, columns, starts, *refs):
    weight_ref, out_ref = refs[count], refs[-1]
    places = lax.axis_size("head")
    share = weight_ref.shape[0] // places
    tiled = out_ref.shape[1] < weight_ref.shape[1]
    for step in [pl.program_id(0)] if tiled else range(weight_ref.shape[1] // columns):
        here = pl.ds(pl.multiple_of(step * columns, columns), columns)
        total = refs[count + 1][:, here] if carried else None
        for i in range(count):
            hops, first_row = starts[i]
            place = lax.rem(lax.axis_index("head") + hops, places)
            rows = pl.ds(pl.multiple_of(place * share + first_row, HEAD_SIZE), refs[i].shape[1])
            term = lax.dot_general(refs[i][...], weight_ref[rows, here], PLAIN, preferred_element_type=jnp.float32)
            total = term if total is None else total + term
        out_ref[:, slice(None) if tiled else here] = total.astype(out_ref.dtype)


def project(pieces, starts, weight, total, name, last=False, columns=512, flops=2**20):
    rows, width = pieces[0].shape[0], weight.shape[1]
    carried = total is not None
    args = [*pieces, weight] + [total] * carried
    if last:
        rest = dict(grid=(width // columns,), out_specs=pl.BlockSpec((rows, columns), lambda n: (0, n)))
    else:
        rest = dict(out_specs=VMEM, input_output_aliases={len(args) - 1: 0} if carried else {})
    return pl.pallas_call(
        functools.partial(project_kernel, len(pieces), carried, columns, starts),
        in_specs=[VMEM] * len(args),
        out_shape=jax.ShapeDtypeStruct((rows, width), jnp.bfloat16 if last else jnp.float32),
        compiler_params=pltpu.CompilerParams(vmem_limit_bytes=6 * 2**20),
        cost_estimate=pl.CostEstimate(flops=flops, bytes_accessed=2**10, transcendentals=0),
        name=name,
        **rest,
    )(*args)


def once_here(value, *others):
    anywhere = pl.BlockSpec(memory_space=pl.ANY)
    return pl.pallas_call(
        lambda *refs: None,
        in_specs=[anywhere] * (1 + len(others)),
        out_specs=anywhere,
        out_shape=jax.ShapeDtypeStruct(value.shape, value.dtype),
        input_output_aliases={0: 0},
        compiler_params=pltpu.CompilerParams(vmem_limit_bytes=2**20),
        cost_estimate=pl.CostEstimate(flops=0, bytes_accessed=0, transcendentals=0),
        name="once_here",
    )(value, *others)


def shards(queries, keys, values, doc_ids, out_weight):
    rows = keys.shape[0]
    shard = lax.axis_index("ctx")
    shard_count = lax.axis_size("ctx")
    places = lax.axis_size("head")
    other_core = [(i, i ^ 1) for i in range(shard_count)]

    def along_ctx(block, pairs):
        return lax.ppermute(block, "ctx", pairs)

    def along_head(block, step):
        return lax.ppermute(block, "head", [(i, (i + step) % places) for i in range(places)])

    own = jnp.concatenate([keys, values], 0)
    two_behind = along_ctx(own, [(i, i + 2) for i in range(shard_count - 2)])
    window = (REACH + 1) * rows
    padded = jnp.concatenate([jnp.full((REACH * rows,), -1, jnp.int32), doc_ids], 0)
    kdoc = lax.dynamic_slice_in_dim(padded, shard * rows, window, 0)
    kdoc = kdoc[None, :]

    splits = (0, 5)
    *state, qdoc, own_again = attend_own(queries, own, kdoc, splits)
    three_behind = along_ctx(own_again, [(i, i + 3) for i in range(1, shard_count - 3, 2)])
    beside = along_ctx(own_again, other_core)
    two_behind = once_here(two_behind, state[0])
    beside_two = along_ctx(two_behind, other_core)
    first_state = attend_two_behind(queries, two_behind, qdoc, kdoc, state[0:2])
    three_behind = once_here(three_behind, beside, beside_two, first_state[0])
    parts = (beside, two_behind, beside_two, three_behind)
    a, = attend_rest(queries, parts, qdoc, kdoc, first_state, splits[0], False)
    a_up = along_head(a, 1)
    a_down = along_head(a, -1)
    b, held = attend_rest(queries, parts, qdoc, kdoc, state[2:4], splits[1], True, out_weight)
    b_up = along_head(b, 1)
    b_down = along_head(b, -1)
    b_row = splits[1] * HEAD_SIZE
    up, down, across = places - 1, 1, places // 2
    total = project([a, b], [(0, 0), (0, b_row)], held, None, "project_own")
    a_up = once_here(a_up, total)
    a_far = along_head(a_up, 1)
    total = project([a_up, a_down], [(up, 0), (down, 0)], held, total, "project_a")
    b_down = once_here(b_down, b_up, total)
    b_far = along_head(b_down, -1)
    total = project([b_up, b_down], [(up, b_row), (down, b_row)], held, total, "project_b")
    total = project([b_far], [(across, b_row)], held, total, "project_b_far")
    return project([a_far], [(across, 0)], held, total, "project_a_far", last=True, columns=1024)


def solution(mesh):
    in_specs = (P("ctx", "head"), P("ctx", "head"), P("ctx", "head"), P(), P(None, "head"))
    out_specs = P("ctx", "head")
    return jax.shard_map(shards, mesh=mesh, in_specs=in_specs, out_specs=out_specs, check_vma=False)
```

profile of v0, /device:TPU:8, one launch (start us, length us, event | category | flops | bytes accessed | tf_op | source)
XLA Modules:
  0.0 66.0 jit_solution(3189201292396812377)
XLA Ops:
  0.0 0.9 %constant_dynamic-update-slice_fusion.1 = bf16[1024,128]{1,0:T(8,128)(2,1)S(1)} fusion(bf16[512,128]{1,0:T(8,128)(2,1)} %param.6), kind=kLoop, calls=%fused_computation.2 | loop fusion | bytes 262144
  0.9 0.9 %constant_dynamic-update-slice_fusion.own_ref = bf16[1024,128]{1,0:T(8,128)(2,1)S(1)} fusion(bf16[1024,128]{1,0:T(8,128)(2,1)S(1)} %constant_dynamic-update-slice_fusion.1, bf16[512,128]{1,0:T(8,128)(2,1)} %param.7), kind=kLoop, calls=%fused_computation.1 | loop fusion | bytes 262144 | tf_op jit(solution)/shard_map/concatenate | solution.py:276
  1.8 3.4 %collective-permute-start.1 = (bf16[1024,128]{1,0:T(8,128)(2,1)S(1)}, bf16[1024,128]{1,0:T(8,128)(2,1)S(1)}, u32[]{:S(2)}, u32[]{:S(2)}) collective-permute-start(bf16[1024,128]{1,0:T(8,128)(2,1)S(1)} %constant_dynamic-update-slice_fusion.own_ref), channel_id=1, source_target_pairs={{0,8},{4,12},{8,16},{12,20},{16,24},{20,28},{24,32},{28,36},{32,40... | collective-permute-start | bytes 786440 | tf_op jit(solution)/shard_map/ppermute | solution.py:271
  6.1 1.2 %copy-done = bf16[512,1024]{1,0:T(8,128)(2,1)S(1)} copy-done((bf16[512,1024]{1,0:T(8,128)(2,1)S(1)}, bf16[512,1024]{1,0:T(8,128)(2,1)}, u32[]{:S(2)}) %copy-start) | copy-done | bytes 1048600
  7.3 2.5 %attend_own.1 = (f32[5,512,128]{2,1,0:T(8,128)S(1)}, f32[5,512,256]{2,1,0:T(8,128)S(1)}, f32[3,512,128]{2,1,0:T(8,128)S(1)}, f32[3,512,256]{2,1,0:T(8,128)S(1)},...) custom-call(bf16[512,1024]{1,0:T(8,128)(2,1)S(1)} %copy-done, ...), custom_call_target="tpu_custom_call" | custom-call | flops 4294967296 | bytes 1048576 | tf_op jit(solution)/shard_map/attend_own/pallas_call | solution.py:162
  9.9 1.3 %collective-permute-start.3 = (bf16[1024,128]{1,0:T(8,128)(2,1)S(1)}, bf16[1024,128]{1,0:T(8,128)(2,1)S(1)}, u32[]{:S(2)}, u32[]{:S(2)}) collective-permute-start(bf16[1024,128]{1,0:T(8,128)(2,1)S(1)} %get-tuple-element.16), channel_id=1, source_target_pairs={{4,16},{12,24},{20,32},{28,40},{36,48},{44,56},{52,64},{60,72},{68... | collective-permute-start | bytes 786440 | tf_op jit(solution)/shard_map/ppermute | solution.py:271
  11.2 2.7 %collective-permute-done.1.refs_0_ = bf16[1024,128]{1,0:T(8,128)(2,1)S(1)} collective-permute-done((bf16[1024,128]{1,0:T(8,128)(2,1)S(1)}, bf16[1024,128]{1,0:T(8,128)(2,1)S(1)}, u32[]{:S(2)}, u32[]{:S(2)}) %collective-permute-start.1) | collective-permute-done | bytes 262176 | tf_op jit(solution)/shard_map/ppermute | solution.py:271
  15.5 4.5 %collective-permute-done.3.refs_0_ = bf16[1024,128]{1,0:T(8,128)(2,1)S(1)} collective-permute-done((bf16[1024,128]{1,0:T(8,128)(2,1)S(1)}, bf16[1024,128]{1,0:T(8,128)(2,1)S(1)}, u32[]{:S(2)}, u32[]{:S(2)}) %collective-permute-start.3) | collective-permute-done | bytes 262176 | tf_op jit(solution)/shard_map/ppermute | solution.py:271
  20.0 2.3 %attend_rest_0.1 = (f32[5,512,128]{2,1,0:T(8,128)S(1)}, f32[5,512,256]{2,1,0:T(8,128)S(1)}, bf16[512,640]{1,0:T(8,128)(2,1)S(1)}) custom-call(s32[2048]{0:T(1024)S(1)} %pad_dynamic-slice_fusion.docs_ref, bf16[512,1024]{1,0:T(8,128)(2,1)S(1)} %copy-done, ...), custom_call_target="tpu_custom_call", output_to_operand_aliasing={{0}: (8, {}), {1}: (9, {})} | custom-call | flops 4294967296 | bytes 1048576 | tf_op jit(solution)/shard_map/attend_rest_0/pallas_call | solution.py:195
  22.3 2.0 %collective-permute-start.4 = (bf16[512,640]{1,0:T(8,128)(2,1)S(1)}, bf16[512,640]{1,0:T(8,128)(2,1)S(1)}, u32[]{:S(2)}, u32[]{:S(2)}) collective-permute-start(bf16[512,640]{1,0:T(8,128)(2,1)S(1)} %get-tuple-element.22.refs_0_), channel_id=1, source_target_pairs={{0,1},{1,2},{2,3},{3,0},{4,5},{5,6},{6,7},{7,4},{8,9},{9,10},{10,1... | collective-permute-start | bytes 1966088 | tf_op jit(solution)/shard_map/ppermute | solution.py:274
  24.3 2.2 %collective-permute-start.8 = (bf16[512,640]{1,0:T(8,128)(2,1)S(1)}, bf16[512,640]{1,0:T(8,128)(2,1)S(1)}, u32[]{:S(2)}, u32[]{:S(2)}) collective-permute-start(bf16[512,640]{1,0:T(8,128)(2,1)S(1)} %get-tuple-element.22.refs_0_), channel_id=1, source_target_pairs={{0,3},{1,0},{2,1},{3,2},{4,7},{5,4},{6,5},{7,6},{8,11},{9,8},{10,9... | collective-permute-start | bytes 1966088 | tf_op jit(solution)/shard_map/ppermute | solution.py:274
  26.5 6.4 %attend_rest_5.1 = (f32[3,512,128]{2,1,0:T(8,128)S(1)}, f32[3,512,256]{2,1,0:T(8,128)S(1)}, bf16[512,384]{1,0:T(8,128)(2,1)S(1)}, bf16[4096,2048]{1,0:T(8,128)(2,1)S(1)}) custom-call(s32[2048]{0:T(1024)S(1)} %pad_dynamic-slice_fusion.docs_ref, bf16[512,1024]{1,0:T(8,128)(2,1)S(1)} %copy-done.1, ...), custom_call_target="tpu_custom_call", output_to_operand_aliasing={{0}: (9, {}), {1}: (10, {})} | custom-call | flops 4294967296 | bytes 1048576 | tf_op jit(solution)/shard_map/attend_rest_5/pallas_call | solution.py:195
  32.9 2.0 %collective-permute-start.6 = (bf16[512,384]{1,0:T(8,128)(2,1)S(1)}, bf16[512,384]{1,0:T(8,128)(2,1)S(1)}, u32[]{:S(2)}, u32[]{:S(2)}) collective-permute-start(bf16[512,384]{1,0:T(8,128)(2,1)S(1)} %get-tuple-element.25.refs_1_), channel_id=1, source_target_pairs={{0,3},{1,0},{2,1},{3,2},{4,7},{5,4},{6,5},{7,6},{8,11},{9,8},{10,9... | collective-permute-start | bytes 1179656 | tf_op jit(solution)/shard_map/ppermute | solution.py:274
  35.0 2.9 %project_own.1.refs_1_.refs_3_ = f32[512,2048]{1,0:T(8,128)S(1)} custom-call(bf16[512,640]{1,0:T(8,128)(2,1)S(1)} %get-tuple-element.22.refs_0_, bf16[512,384]{1,0:T(8,128)(2,1)S(1)} %get-tuple-element.25.refs_1_, bf16[4096,2048]{1,0:T(8,128)(2,1)S(1)} %get-tuple-element.26.refs_2_.refs_1_), custom_call_target="tpu_custom_call" | custom-call | flops 1048576 | bytes 1024 | tf_op jit(solution)/shard_map/project_own/pallas_call | solution.py:238
  37.9 4.2 %collective-permute-done.4.refs_0_ = bf16[512,640]{1,0:T(8,128)(2,1)S(1)} collective-permute-done((bf16[512,640]{1,0:T(8,128)(2,1)S(1)}, bf16[512,640]{1,0:T(8,128)(2,1)S(1)}, u32[]{:S(2)}, u32[]{:S(2)}) %collective-permute-start.4) | collective-permute-done | bytes 655392 | tf_op jit(solution)/shard_map/ppermute | solution.py:274
  42.0 3.7 %project_a.1.refs_2_.refs_3_ = f32[512,2048]{1,0:T(8,128)S(1)} custom-call(bf16[512,640]{1,0:T(8,128)(2,1)S(1)} %once_here.6.refs_0_, bf16[512,640]{1,0:T(8,128)(2,1)S(1)} %collective-permute-done.8.refs_1_, bf16[4096,2048]{1,0:T(8,128)(2,1)S(1)} %get-tuple-element.26.refs_2_.refs_1_, ...), custom_call_target="tpu_custom_call", output_to_operand_aliasing={{}: (3, {})} | custom-call | flops 1048576 | bytes 1024 | tf_op jit(solution)/shard_map/project_a/pallas_call | solution.py:238
  45.7 2.7 %collective-permute-done.6.refs_0_ = bf16[512,384]{1,0:T(8,128)(2,1)S(1)} collective-permute-done((bf16[512,384]{1,0:T(8,128)(2,1)S(1)}, bf16[512,384]{1,0:T(8,128)(2,1)S(1)}, u32[]{:S(2)}, u32[]{:S(2)}) %collective-permute-start.6) | collective-permute-done | bytes 393248 | tf_op jit(solution)/shard_map/ppermute | solution.py:274
  48.4 2.0 %collective-permute-done.7.refs_1_.refs_0_ = bf16[512,384]{1,0:T(8,128)(2,1)S(1)} collective-permute-done((bf16[512,384]{1,0:T(8,128)(2,1)S(1)}, bf16[512,384]{1,0:T(8,128)(2,1)S(1)}, u32[]{:S(2)}, u32[]{:S(2)}) %collective-permute-start.7) | collective-permute-done | bytes 393248 | tf_op jit(solution)/shard_map/ppermute | solution.py:274
  50.5 2.0 %collective-permute-start.9 = (bf16[512,384]{1,0:T(8,128)(2,1)S(1)}, bf16[512,384]{1,0:T(8,128)(2,1)S(1)}, u32[]{:S(2)}, u32[]{:S(2)}) collective-permute-start(bf16[512,384]{1,0:T(8,128)(2,1)S(1)} %once_here.7.refs_1_), channel_id=1, source_target_pairs={{0,3},{1,0},{2,1},{3,2},{4,7},{5,4},{6,5},{7,6},{8,11},{9,8},{10,9... | collective-permute-start | bytes 1179656 | tf_op jit(solution)/shard_map/ppermute | solution.py:274
  52.5 2.5 %project_b.1.refs_2_ = f32[512,2048]{1,0:T(8,128)S(1)} custom-call(bf16[512,384]{1,0:T(8,128)(2,1)S(1)} %collective-permute-done.7.refs_1_.refs_0_, bf16[512,384]{1,0:T(8,128)(2,1)S(1)} %once_here.7.refs_1_, bf16[4096,2048]{1,0:T(8,128)(2,1)S(1)} %get-tuple-element.26.refs_2_.refs_1_, ...), custom_call_target="tpu_custom_call", output_to_operand_aliasing={{}: (3, {})} | custom-call | flops 1048576 | bytes 1024 | tf_op jit(solution)/shard_map/project_b/pallas_call | solution.py:238
  55.0 3.8 %collective-permute-done.9.refs_0_ = bf16[512,384]{1,0:T(8,128)(2,1)S(1)} collective-permute-done((bf16[512,384]{1,0:T(8,128)(2,1)S(1)}, bf16[512,384]{1,0:T(8,128)(2,1)S(1)}, u32[]{:S(2)}, u32[]{:S(2)}) %collective-permute-start.9) | collective-permute-done | bytes 393248 | tf_op jit(solution)/shard_map/ppermute | solution.py:274
  58.8 1.4 %project_b_far.1.refs_2_ = f32[512,2048]{1,0:T(8,128)S(1)} custom-call(bf16[512,384]{1,0:T(8,128)(2,1)S(1)} %collective-permute-done.9.refs_0_, bf16[4096,2048]{1,0:T(8,128)(2,1)S(1)} %get-tuple-element.26.refs_2_.refs_1_, f32[512,2048]{1,0:T(8,128)S(1)} %project_b.1.refs_2_), custom_call_target="tpu_custom_call", output_to_operand_aliasing={{}: (2, {})} | custom-call | flops 1048576 | bytes 1024 | tf_op jit(solution)/shard_map/project_b_far/pallas_call | solution.py:238
  60.2 2.7 %collective-permute-done.5.refs_0_ = bf16[512,640]{1,0:T(8,128)(2,1)S(1)} collective-permute-done((bf16[512,640]{1,0:T(8,128)(2,1)S(1)}, bf16[512,640]{1,0:T(8,128)(2,1)S(1)}, u32[]{:S(2)}, u32[]{:S(2)}) %collective-permute-start.5) | collective-permute-done | bytes 655392 | tf_op jit(solution)/shard_map/ppermute | solution.py:274
  63.0 3.0 %project_a_far.1 = bf16[512,2048]{1,0:T(8,128)(2,1)} custom-call(bf16[512,640]{1,0:T(8,128)(2,1)S(1)} %collective-permute-done.5.refs_0_, bf16[4096,2048]{1,0:T(8,128)(2,1)S(1)} %get-tuple-element.26.refs_2_.refs_1_, f32[512,2048]{1,0:T(8,128)S(1)} %project_b_far.1.refs_2_), custom_call_target="tpu_custom_call" | custom-call | flops 1048576 | bytes 1024 | tf_op jit(solution)/shard_map/project_a_far/pallas_call | solution.py:238
  (16 shorter events, 2.6 us)
Async XLA Ops:
  1.8 12.0 %collective-permute-start.1 = (bf16[1024,128]{1,0:T(8,128)(2,1)S(1)}, bf16[1024,128]{1,0:T(8,128)(2,1)S(1)}, u32[]{:S(2)}, u32[]{:S(2)}) collective-permute-start(bf16[1024,128]{1,0:T(8,128)(2,1)S(1)} %constant_dynamic-update-slice_fusion.own_ref), channel_id=1, source_target_pairs={{0,8},{4,12},{8,16},{12,20},{16,24},{20,28},{24,32},{28,36},{32,40... | collective-permute-start | bytes 786440 | tf_op jit(solution)/shard_map/ppermute | solution.py:271
  6.1 1.2 %copy-start = (bf16[512,1024]{1,0:T(8,128)(2,1)S(1)}, bf16[512,1024]{1,0:T(8,128)(2,1)}, u32[]{:S(2)}) copy-start(bf16[512,1024]{1,0:T(8,128)(2,1)} %q_ref.7) | copy-start | bytes 3145732
  9.8 5.7 %collective-permute-start = (bf16[1024,128]{1,0:T(8,128)(2,1)S(1)}, bf16[1024,128]{1,0:T(8,128)(2,1)S(1)}, u32[]{:S(2)}, u32[]{:S(2)}) collective-permute-start(bf16[1024,128]{1,0:T(8,128)(2,1)S(1)} %get-tuple-element.16), channel_id=1, source_target_pairs={{0,4},{4,0},{8,12},{12,8},{16,20},{20,16},{24,28},{28,24},{32,36},... | collective-permute-start | bytes 786440 | tf_op jit(solution)/shard_map/ppermute | solution.py:271
  9.9 10.1 %collective-permute-start.3 = (bf16[1024,128]{1,0:T(8,128)(2,1)S(1)}, bf16[1024,128]{1,0:T(8,128)(2,1)S(1)}, u32[]{:S(2)}, u32[]{:S(2)}) collective-permute-start(bf16[1024,128]{1,0:T(8,128)(2,1)S(1)} %get-tuple-element.16), channel_id=1, source_target_pairs={{4,16},{12,24},{20,32},{28,40},{36,48},{44,56},{52,64},{60,72},{68... | collective-permute-start | bytes 786440 | tf_op jit(solution)/shard_map/ppermute | solution.py:271
  13.9 6.1 %collective-permute-start.2 = (bf16[1024,128]{1,0:T(8,128)(2,1)S(1)}, bf16[1024,128]{1,0:T(8,128)(2,1)S(1)}, u32[]{:S(2)}, u32[]{:S(2)}) collective-permute-start(bf16[1024,128]{1,0:T(8,128)(2,1)S(1)} %once_here.4.k2_ref), channel_id=1, source_target_pairs={{0,4},{4,0},{8,12},{12,8},{16,20},{20,16},{24,28},{28,24},{32,36},... | collective-permute-start | bytes 786440 | tf_op jit(solution)/shard_map/ppermute | solution.py:271
  20.0 6.5 %copy-start.1 = (bf16[512,1024]{1,0:T(8,128)(2,1)S(1)}, bf16[512,1024]{1,0:T(8,128)(2,1)}, u32[]{:S(2)}) copy-start(bf16[512,1024]{1,0:T(8,128)(2,1)} %q_ref.7) | copy-start | bytes 3145732
  22.3 19.8 %collective-permute-start.4 = (bf16[512,640]{1,0:T(8,128)(2,1)S(1)}, bf16[512,640]{1,0:T(8,128)(2,1)S(1)}, u32[]{:S(2)}, u32[]{:S(2)}) collective-permute-start(bf16[512,640]{1,0:T(8,128)(2,1)S(1)} %get-tuple-element.22.refs_0_), channel_id=1, source_target_pairs={{0,1},{1,2},{2,3},{3,0},{4,5},{5,6},{6,7},{7,4},{8,9},{9,10},{10,1... | collective-permute-start | bytes 1966088 | tf_op jit(solution)/shard_map/ppermute | solution.py:274
  24.3 17.8 %collective-permute-start.8 = (bf16[512,640]{1,0:T(8,128)(2,1)S(1)}, bf16[512,640]{1,0:T(8,128)(2,1)S(1)}, u32[]{:S(2)}, u32[]{:S(2)}) collective-permute-start(bf16[512,640]{1,0:T(8,128)(2,1)S(1)} %get-tuple-element.22.refs_0_), channel_id=1, source_target_pairs={{0,3},{1,0},{2,1},{3,2},{4,7},{5,4},{6,5},{7,6},{8,11},{9,8},{10,9... | collective-permute-start | bytes 1966088 | tf_op jit(solution)/shard_map/ppermute | solution.py:274
  32.9 15.5 %collective-permute-start.6 = (bf16[512,384]{1,0:T(8,128)(2,1)S(1)}, bf16[512,384]{1,0:T(8,128)(2,1)S(1)}, u32[]{:S(2)}, u32[]{:S(2)}) collective-permute-start(bf16[512,384]{1,0:T(8,128)(2,1)S(1)} %get-tuple-element.25.refs_1_), channel_id=1, source_target_pairs={{0,3},{1,0},{2,1},{3,2},{4,7},{5,4},{6,5},{7,6},{8,11},{9,8},{10,9... | collective-permute-start | bytes 1179656 | tf_op jit(solution)/shard_map/ppermute | solution.py:274
  34.9 15.5 %collective-permute-start.7 = (bf16[512,384]{1,0:T(8,128)(2,1)S(1)}, bf16[512,384]{1,0:T(8,128)(2,1)S(1)}, u32[]{:S(2)}, u32[]{:S(2)}) collective-permute-start(bf16[512,384]{1,0:T(8,128)(2,1)S(1)} %get-tuple-element.25.refs_1_), channel_id=1, source_target_pairs={{0,1},{1,2},{2,3},{3,0},{4,5},{5,6},{6,7},{7,4},{8,9},{9,10},{10,1... | collective-permute-start | bytes 1179656 | tf_op jit(solution)/shard_map/ppermute | solution.py:274
  42.0 20.9 %collective-permute-start.5 = (bf16[512,640]{1,0:T(8,128)(2,1)S(1)}, bf16[512,640]{1,0:T(8,128)(2,1)S(1)}, u32[]{:S(2)}, u32[]{:S(2)}) collective-permute-start(bf16[512,640]{1,0:T(8,128)(2,1)S(1)} %once_here.6.refs_0_), channel_id=1, source_target_pairs={{0,1},{1,2},{2,3},{3,0},{4,5},{5,6},{6,7},{7,4},{8,9},{9,10},{10,1... | collective-permute-start | bytes 1966088 | tf_op jit(solution)/shard_map/ppermute | solution.py:274
  50.5 8.3 %collective-permute-start.9 = (bf16[512,384]{1,0:T(8,128)(2,1)S(1)}, bf16[512,384]{1,0:T(8,128)(2,1)S(1)}, u32[]{:S(2)}, u32[]{:S(2)}) collective-permute-start(bf16[512,384]{1,0:T(8,128)(2,1)S(1)} %once_here.7.refs_1_), channel_id=1, source_target_pairs={{0,3},{1,0},{2,1},{3,2},{4,7},{5,4},{6,5},{7,6},{8,11},{9,8},{10,9... | collective-permute-start | bytes 1179656 | tf_op jit(solution)/shard_map/ppermute | solution.py:274
where the time goes:
time: 67 us; the launch traced here: 66 us
  Pallas kernels  25.4 us (38%)
  waiting for transfers between devices  22.6 us (34%)
  starting transfers between devices  14 us (21%)
  local copies, waits for them, and re-layouts  3.87 us (6%)
    ppermute x6, waiting for transfers between devices, along_head(): lax.ppermute(block, 'head', [(i, (i + step) % places) for i in range(plac...  15.4 us
    pallas_call x5, Pallas kernels, project(): pl.pallas_call(functools.partial(project_kernel, len(pieces), carried, co...  13.5 us
    pallas_call x2, Pallas kernels, attend_rest(): pl.pallas_call(functools.partial(rest_kernel, first_head, heads, fetches,...  8.71 us
    ppermute x6, starting transfers between devices, along_head(): lax.ppermute(block, 'head', [(i, (i + step) % places) for i in range(plac...  8.31 us
    ppermute x4, waiting for transfers between devices, along_ctx(): return lax.ppermute(block, 'ctx', pairs)  7.2 us
    ppermute x4, starting transfers between devices, along_ctx(): return lax.ppermute(block, 'ctx', pairs)  5.65 us
    pallas_call x1, Pallas kernels, attend_own(): pl.pallas_call(functools.partial(own_kernel, splits), in_specs=[VMEM] * 3...  2.5 us
    unnamed x5, local copies, waits for them, and re-layouts  2.14 us
  transfers between devices with their start and end apart: 10, of which 7 were waited for; matrix products, arithmetic and copies ran while one was open for 1% of the time, Pallas kernels for 31%

commit v1 on v0

--- a/solution.py
+++ b/solution.py
@@ -210,13 +210,13 @@
     )(kdoc.reshape(-1), queries, *parts, qdoc, kdoc, *[weight] * fetches, *state)[2:]
 
 
-def project_kernel(count, carried, columns, starts, *refs):
-    weight_ref, out_ref = refs[count], refs[-1]
+def project_kernel(count, carried, last, columns, starts, *refs):
+    weight_ref, out_ref = refs[count], refs[count + 1 + carried]
     places = lax.axis_size("head")
     share = weight_ref.shape[0] // places
-    tiled = out_ref.shape[1] < weight_ref.shape[1]
-    for step in [pl.program_id(0)] if tiled else range(weight_ref.shape[1] // columns):
-        here = pl.ds(pl.multiple_of(step * columns, columns), columns)
+    copies = []
+    for step in range(weight_ref.shape[1] // columns):
+        here = slice(step * columns, (step + 1) * columns)
         total = refs[count + 1][:, here] if carried else None
         for i in range(count):
             hops, first_row = starts[i]
@@ -224,19 +224,31 @@
             rows = pl.ds(pl.multiple_of(place * share + first_row, HEAD_SIZE), refs[i].shape[1])
             term = lax.dot_general(refs[i][...], weight_ref[rows, here], PLAIN, preferred_element_type=jnp.float32)
             total = term if total is None else total + term
-        out_ref[:, slice(None) if tiled else here] = total.astype(out_ref.dtype)
+        if last:
+            tile_ref, sems = refs[-2], refs[-1]
+            tile_ref[step] = total.astype(out_ref.dtype)
+            copies.append(pltpu.make_async_copy(tile_ref.at[step], out_ref.at[:, here], sems.at[step]))
+            copies[-1].start()
+        else:
+            out_ref[:, here] = total
+    for copy in copies:
+        copy.wait()
 
 
 def project(pieces, starts, weight, total, name, last=False, columns=512, flops=2**20):
     rows, width = pieces[0].shape[0], weight.shape[1]
     carried = total is not None
     args = [*pieces, weight] + [total] * carried
+    tiles = width // columns
     if last:
-        rest = dict(grid=(width // columns,), out_specs=pl.BlockSpec((rows, columns), lambda n: (0, n)))
+        rest = dict(
+            out_specs=pl.BlockSpec(memory_space=pl.ANY),
+            scratch_shapes=[pltpu.VMEM((tiles, rows, columns), jnp.bfloat16), pltpu.SemaphoreType.DMA((tiles,))],
+        )
     else:
         rest = dict(out_specs=VMEM, input_output_aliases={len(args) - 1: 0} if carried else {})
     return pl.pallas_call(
-        functools.partial(project_kernel, len(pieces), carried, columns, starts),
+        functools.partial(project_kernel, len(pieces), carried, last, columns, starts),
         in_specs=[VMEM] * len(args),
         out_shape=jax.ShapeDtypeStruct((rows, width), jnp.bfloat16 if last else jnp.float32),
         compiler_params=pltpu.CompilerParams(vmem_limit_bytes=6 * 2**20),
@@ -275,6 +287,7 @@
 
     own = jnp.concatenate([keys, values], 0)
     two_behind = along_ctx(own, [(i, i + 2) for i in range(shard_count - 2)])
+    three_behind = along_ctx(own, [(i, i + 3) for i in range(1, shard_count - 3, 2)])
     window = (REACH + 1) * rows
     padded = jnp.concatenate([jnp.full((REACH * rows,), -1, jnp.int32), doc_ids], 0)
     kdoc = lax.dynamic_slice_in_dim(padded, shard * rows, window, 0)
@@ -282,7 +295,6 @@
 
     splits = (0, 5)
     *state, qdoc, own_again = attend_own(queries, own, kdoc, splits)
-    three_behind = along_ctx(own_again, [(i, i + 3) for i in range(1, shard_count - 3, 2)])
     beside = along_ctx(own_again, other_core)
     two_behind = once_here(two_behind, state[0])
     beside_two = along_ctx(two_behind, other_core)
@@ -305,7 +317,7 @@
     b_far = along_head(b_down, -1)
     total = project([b_up, b_down], [(up, b_row), (down, b_row)], held, total, "project_b")
     total = project([b_far], [(across, b_row)], held, total, "project_b_far")
-    return project([a_far], [(across, 0)], held, total, "project_a_far", last=True, columns=1024)
+    return project([a_far], [(across, 0)], held, total, "project_a_far", last=True)
 
 
 def solution(mesh):

time: 67 us -> 66.2 us (0.988)
  the two profiles are of different devices: /device:TPU:8 before, /device:TPU:9 now
where the time goes in v1:
time: 66.2 us; the launch traced here: 65.2 us
  Pallas kernels  28.8 us (44%)
  starting transfers between devices  16.2 us (24%)
  waiting for transfers between devices  16.1 us (24%)
  local copies, waits for them, and re-layouts  3.87 us (6%)
    ppermute x6, waiting for transfers between devices, along_head(): lax.ppermute(block, 'head', [(i, (i + step) % places) for i in range(plac...  16.1 us
    pallas_call x5, Pallas kernels, project(): pl.pallas_call(functools.partial(project_kernel, len(pieces), carried, la...  13.1 us
    pallas_call x2, Pallas kernels, attend_rest(): pl.pallas_call(functools.partial(rest_kernel, first_head, heads, fetches,...  9.87 us
    ppermute x4, starting transfers between devices, along_ctx(): return lax.ppermute(block, 'ctx', pairs)  9.29 us
    ppermute x6, starting transfers between devices, along_head(): lax.ppermute(block, 'head', [(i, (i + step) % places) for i in range(plac...  6.87 us
    pallas_call x1, Pallas kernels, attend_two_behind(): pl.pallas_call(two_behind_kernel, in_specs=[SMEM] + [VMEM] * 6, out_specs...  3.25 us
    pallas_call x1, Pallas kernels, attend_own(): pl.pallas_call(functools.partial(own_kernel, splits), in_specs=[VMEM] * 3...  2.51 us
    unnamed x5, local copies, waits for them, and re-layouts  2.14 us
  transfers between devices with their start and end apart: 10, of which 5 were waited for; matrix products, arithmetic and copies ran while one was open for 1% of the time, Pallas kernels for 35%

profile of v1, /device:TPU:9, one launch (start us, length us, event | category | flops | bytes accessed | tf_op | source)
XLA Modules:
  0.0 65.2 jit_solution(4629417269799501904)
XLA Ops:
  0.0 0.9 %constant_dynamic-update-slice_fusion.1 = bf16[1024,128]{1,0:T(8,128)(2,1)S(1)} fusion(bf16[512,128]{1,0:T(8,128)(2,1)} %param.6), kind=kLoop, calls=%fused_computation.2 | loop fusion | bytes 262144
  0.9 0.9 %constant_dynamic-update-slice_fusion.own_ref = bf16[1024,128]{1,0:T(8,128)(2,1)S(1)} fusion(bf16[1024,128]{1,0:T(8,128)(2,1)S(1)} %constant_dynamic-update-slice_fusion.1, bf16[512,128]{1,0:T(8,128)(2,1)} %param.7), kind=kLoop, calls=%fused_computation.1 | loop fusion | bytes 262144 | tf_op jit(solution)/shard_map/concatenate | solution.py:288
  1.8 3.1 %collective-permute-start.1 = (bf16[1024,128]{1,0:T(8,128)(2,1)S(1)}, bf16[1024,128]{1,0:T(8,128)(2,1)S(1)}, u32[]{:S(2)}, u32[]{:S(2)}) collective-permute-start(bf16[1024,128]{1,0:T(8,128)(2,1)S(1)} %constant_dynamic-update-slice_fusion.own_ref), channel_id=1, source_target_pairs={{0,8},{4,12},{8,16},{12,20},{16,24},{20,28},{24,32},{28,36},{32,40... | collective-permute-start | bytes 786440 | tf_op jit(solution)/shard_map/ppermute | solution.py:283
  5.0 5.2 %collective-permute-start.3 = (bf16[1024,128]{1,0:T(8,128)(2,1)S(1)}, bf16[1024,128]{1,0:T(8,128)(2,1)S(1)}, u32[]{:S(2)}, u32[]{:S(2)}) collective-permute-start(bf16[1024,128]{1,0:T(8,128)(2,1)S(1)} %constant_dynamic-update-slice_fusion.own_ref), channel_id=1, source_target_pairs={{4,16},{12,24},{20,32},{28,40},{36,48},{44,56},{52,64},{60,72},{68... | collective-permute-start | bytes 786440 | tf_op jit(solution)/shard_map/ppermute | solution.py:283
  10.2 0.8 %pad_dynamic-slice_fusion.docs_ref = s32[2048]{0:T(1024)S(1)} fusion(s32[]{:T(128)S(6)} %select_n.3, s32[16384]{0:T(1024)} %param.8), kind=kLoop, calls=%fused_computation | loop fusion | bytes 73732 | tf_op jit(solution)/shard_map/dynamic_slice | solution.py:293
  11.0 1.2 %copy-done = bf16[512,1024]{1,0:T(8,128)(2,1)S(1)} copy-done((bf16[512,1024]{1,0:T(8,128)(2,1)S(1)}, bf16[512,1024]{1,0:T(8,128)(2,1)}, u32[]{:S(2)}) %copy-start) | copy-done | bytes 1048600
  12.2 2.5 %attend_own.1 = (f32[5,512,128]{2,1,0:T(8,128)S(1)}, f32[5,512,256]{2,1,0:T(8,128)S(1)}, f32[3,512,128]{2,1,0:T(8,128)S(1)}, f32[3,512,256]{2,1,0:T(8,128)S(1)},...) custom-call(bf16[512,1024]{1,0:T(8,128)(2,1)S(1)} %copy-done, ...), custom_call_target="tpu_custom_call" | custom-call | flops 4294967296 | bytes 1048576 | tf_op jit(solution)/shard_map/attend_own/pallas_call | solution.py:162
  14.8 0.9 %collective-permute-start.2 = (bf16[1024,128]{1,0:T(8,128)(2,1)S(1)}, bf16[1024,128]{1,0:T(8,128)(2,1)S(1)}, u32[]{:S(2)}, u32[]{:S(2)}) collective-permute-start(bf16[1024,128]{1,0:T(8,128)(2,1)S(1)} %once_here.4.k2_ref), channel_id=1, source_target_pairs={{0,4},{4,0},{8,12},{12,8},{16,20},{20,16},{24,28},{28,24},{32,36},... | collective-permute-start | bytes 786440 | tf_op jit(solution)/shard_map/ppermute | solution.py:283
  15.7 3.2 %attend_two_behind.1 = (f32[5,512,128]{2,1,0:T(8,128)S(1)}, f32[5,512,256]{2,1,0:T(8,128)S(1)}) custom-call(s32[2048]{0:T(1024)S(1)} %pad_dynamic-slice_fusion.docs_ref, bf16[512,1024]{1,0:T(8,128)(2,1)S(1)} %copy-done, bf16[1024,128]{1,0:T(8,128)(2,1)S(1)} %once_here.4.k2_ref, ...), custom_call_target="tpu_custom_call", output_to_operand_aliasing={{0}: (5, {}), {1}: (6, {})} | custom-call | flops 4294967296 | bytes 1048576 | tf_op jit(solution)/shard_map/attend_two_behind/pallas_call | solution.py:177
  19.0 3.4 %attend_rest_0.1 = (f32[5,512,128]{2,1,0:T(8,128)S(1)}, f32[5,512,256]{2,1,0:T(8,128)S(1)}, bf16[512,640]{1,0:T(8,128)(2,1)S(1)}) custom-call(s32[2048]{0:T(1024)S(1)} %pad_dynamic-slice_fusion.docs_ref, bf16[512,1024]{1,0:T(8,128)(2,1)S(1)} %copy-done, ...), custom_call_target="tpu_custom_call", output_to_operand_aliasing={{0}: (8, {}), {1}: (9, {})} | custom-call | flops 4294967296 | bytes 1048576 | tf_op jit(solution)/shard_map/attend_rest_0/pallas_call | solution.py:195
  22.5 1.7 %collective-permute-start.4 = (bf16[512,640]{1,0:T(8,128)(2,1)S(1)}, bf16[512,640]{1,0:T(8,128)(2,1)S(1)}, u32[]{:S(2)}, u32[]{:S(2)}) collective-permute-start(bf16[512,640]{1,0:T(8,128)(2,1)S(1)} %get-tuple-element.22.refs_0_), channel_id=1, source_target_pairs={{0,1},{1,2},{2,3},{3,0},{4,5},{5,6},{6,7},{7,4},{8,9},{9,10},{10,1... | collective-permute-start | bytes 1966088 | tf_op jit(solution)/shard_map/ppermute | solution.py:286
  24.2 2.2 %collective-permute-start.8 = (bf16[512,640]{1,0:T(8,128)(2,1)S(1)}, bf16[512,640]{1,0:T(8,128)(2,1)S(1)}, u32[]{:S(2)}, u32[]{:S(2)}) collective-permute-start(bf16[512,640]{1,0:T(8,128)(2,1)S(1)} %get-tuple-element.22.refs_0_), channel_id=1, source_target_pairs={{0,3},{1,0},{2,1},{3,2},{4,7},{5,4},{6,5},{7,6},{8,11},{9,8},{10,9... | collective-permute-start | bytes 1966088 | tf_op jit(solution)/shard_map/ppermute | solution.py:286
  26.4 6.4 %attend_rest_5.1 = (f32[3,512,128]{2,1,0:T(8,128)S(1)}, f32[3,512,256]{2,1,0:T(8,128)S(1)}, bf16[512,384]{1,0:T(8,128)(2,1)S(1)}, bf16[4096,2048]{1,0:T(8,128)(2,1)S(1)}) custom-call(s32[2048]{0:T(1024)S(1)} %pad_dynamic-slice_fusion.docs_ref, bf16[512,1024]{1,0:T(8,128)(2,1)S(1)} %copy-done.1, ...), custom_call_target="tpu_custom_call", output_to_operand_aliasing={{0}: (9, {}), {1}: (10, {})} | custom-call | flops 4294967296 | bytes 1048576 | tf_op jit(solution)/shard_map/attend_rest_5/pallas_call | solution.py:195
  32.8 1.5 %collective-permute-start.6 = (bf16[512,384]{1,0:T(8,128)(2,1)S(1)}, bf16[512,384]{1,0:T(8,128)(2,1)S(1)}, u32[]{:S(2)}, u32[]{:S(2)}) collective-permute-start(bf16[512,384]{1,0:T(8,128)(2,1)S(1)} %get-tuple-element.25.refs_1_), channel_id=1, source_target_pairs={{0,3},{1,0},{2,1},{3,2},{4,7},{5,4},{6,5},{7,6},{8,11},{9,8},{10,9... | collective-permute-start | bytes 1179656 | tf_op jit(solution)/shard_map/ppermute | solution.py:286
  34.4 2.9 %project_own.1.refs_1_.refs_3_ = f32[512,2048]{1,0:T(8,128)S(1)} custom-call(bf16[512,640]{1,0:T(8,128)(2,1)S(1)} %get-tuple-element.22.refs_0_, bf16[512,384]{1,0:T(8,128)(2,1)S(1)} %get-tuple-element.25.refs_1_, bf16[4096,2048]{1,0:T(8,128)(2,1)S(1)} %get-tuple-element.26.refs_2_.refs_1_), custom_call_target="tpu_custom_call" | custom-call | flops 1048576 | bytes 1024 | tf_op jit(solution)/shard_map/project_own/pallas_call | solution.py:250
  37.2 4.4 %collective-permute-done.4.refs_0_ = bf16[512,640]{1,0:T(8,128)(2,1)S(1)} collective-permute-done((bf16[512,640]{1,0:T(8,128)(2,1)S(1)}, bf16[512,640]{1,0:T(8,128)(2,1)S(1)}, u32[]{:S(2)}, u32[]{:S(2)}) %collective-permute-start.4) | collective-permute-done | bytes 655392 | tf_op jit(solution)/shard_map/ppermute | solution.py:286
  41.6 3.7 %project_a.1.refs_2_.refs_3_ = f32[512,2048]{1,0:T(8,128)S(1)} custom-call(bf16[512,640]{1,0:T(8,128)(2,1)S(1)} %once_here.6.refs_0_, bf16[512,640]{1,0:T(8,128)(2,1)S(1)} %collective-permute-done.8.refs_1_, bf16[4096,2048]{1,0:T(8,128)(2,1)S(1)} %get-tuple-element.26.refs_2_.refs_1_, ...), custom_call_target="tpu_custom_call", output_to_operand_aliasing={{}: (3, {})} | custom-call | flops 1048576 | bytes 1024 | tf_op jit(solution)/shard_map/project_a/pallas_call | solution.py:250
  45.3 3.2 %collective-permute-done.6.refs_0_ = bf16[512,384]{1,0:T(8,128)(2,1)S(1)} collective-permute-done((bf16[512,384]{1,0:T(8,128)(2,1)S(1)}, bf16[512,384]{1,0:T(8,128)(2,1)S(1)}, u32[]{:S(2)}, u32[]{:S(2)}) %collective-permute-start.6) | collective-permute-done | bytes 393248 | tf_op jit(solution)/shard_map/ppermute | solution.py:286
  48.5 1.5 %collective-permute-done.7.refs_1_.refs_0_ = bf16[512,384]{1,0:T(8,128)(2,1)S(1)} collective-permute-done((bf16[512,384]{1,0:T(8,128)(2,1)S(1)}, bf16[512,384]{1,0:T(8,128)(2,1)S(1)}, u32[]{:S(2)}, u32[]{:S(2)}) %collective-permute-start.7) | collective-permute-done | bytes 393248 | tf_op jit(solution)/shard_map/ppermute | solution.py:286
  50.1 1.4 %collective-permute-start.9 = (bf16[512,384]{1,0:T(8,128)(2,1)S(1)}, bf16[512,384]{1,0:T(8,128)(2,1)S(1)}, u32[]{:S(2)}, u32[]{:S(2)}) collective-permute-start(bf16[512,384]{1,0:T(8,128)(2,1)S(1)} %once_here.7.refs_1_), channel_id=1, source_target_pairs={{0,3},{1,0},{2,1},{3,2},{4,7},{5,4},{6,5},{7,6},{8,11},{9,8},{10,9... | collective-permute-start | bytes 1179656 | tf_op jit(solution)/shard_map/ppermute | solution.py:286
  51.5 2.5 %project_b.1.refs_2_ = f32[512,2048]{1,0:T(8,128)S(1)} custom-call(bf16[512,384]{1,0:T(8,128)(2,1)S(1)} %collective-permute-done.7.refs_1_.refs_0_, bf16[512,384]{1,0:T(8,128)(2,1)S(1)} %once_here.7.refs_1_, bf16[4096,2048]{1,0:T(8,128)(2,1)S(1)} %get-tuple-element.26.refs_2_.refs_1_, ...), custom_call_target="tpu_custom_call", output_to_operand_aliasing={{}: (3, {})} | custom-call | flops 1048576 | bytes 1024 | tf_op jit(solution)/shard_map/project_b/pallas_call | solution.py:250
  54.0 6.4 %collective-permute-done.9.refs_0_ = bf16[512,384]{1,0:T(8,128)(2,1)S(1)} collective-permute-done((bf16[512,384]{1,0:T(8,128)(2,1)S(1)}, bf16[512,384]{1,0:T(8,128)(2,1)S(1)}, u32[]{:S(2)}, u32[]{:S(2)}) %collective-permute-start.9) | collective-permute-done | bytes 393248 | tf_op jit(solution)/shard_map/ppermute | solution.py:286
  60.4 1.4 %project_b_far.1.refs_2_ = f32[512,2048]{1,0:T(8,128)S(1)} custom-call(bf16[512,384]{1,0:T(8,128)(2,1)S(1)} %collective-permute-done.9.refs_0_, bf16[4096,2048]{1,0:T(8,128)(2,1)S(1)} %get-tuple-element.26.refs_2_.refs_1_, f32[512,2048]{1,0:T(8,128)S(1)} %project_b.1.refs_2_), custom_call_target="tpu_custom_call", output_to_operand_aliasing={{}: (2, {})} | custom-call | flops 1048576 | bytes 1024 | tf_op jit(solution)/shard_map/project_b_far/pallas_call | solution.py:250
  62.4 2.7 %project_a_far.1 = bf16[512,2048]{1,0:T(8,128)(2,1)} custom-call(bf16[512,640]{1,0:T(8,128)(2,1)S(1)} %collective-permute-done.5.refs_0_, bf16[4096,2048]{1,0:T(8,128)(2,1)S(1)} %get-tuple-element.26.refs_2_.refs_1_, f32[512,2048]{1,0:T(8,128)S(1)} %project_b_far.1.refs_2_), custom_call_target="tpu_custom_call" | custom-call | flops 1048576 | bytes 1024 | tf_op jit(solution)/shard_map/project_a_far/pallas_call | solution.py:250
  (16 shorter events, 0.7 us)
Async XLA Ops:
  1.8 13.0 %collective-permute-start.1 = (bf16[1024,128]{1,0:T(8,128)(2,1)S(1)}, bf16[1024,128]{1,0:T(8,128)(2,1)S(1)}, u32[]{:S(2)}, u32[]{:S(2)}) collective-permute-start(bf16[1024,128]{1,0:T(8,128)(2,1)S(1)} %constant_dynamic-update-slice_fusion.own_ref), channel_id=1, source_target_pairs={{0,8},{4,12},{8,16},{12,20},{16,24},{20,28},{24,32},{28,36},{32,40... | collective-permute-start | bytes 786440 | tf_op jit(solution)/shard_map/ppermute | solution.py:283
  5.0 14.0 %collective-permute-start.3 = (bf16[1024,128]{1,0:T(8,128)(2,1)S(1)}, bf16[1024,128]{1,0:T(8,128)(2,1)S(1)}, u32[]{:S(2)}, u32[]{:S(2)}) collective-permute-start(bf16[1024,128]{1,0:T(8,128)(2,1)S(1)} %constant_dynamic-update-slice_fusion.own_ref), channel_id=1, source_target_pairs={{4,16},{12,24},{20,32},{28,40},{36,48},{44,56},{52,64},{60,72},{68... | collective-permute-start | bytes 786440 | tf_op jit(solution)/shard_map/ppermute | solution.py:283
  11.0 1.2 %copy-start = (bf16[512,1024]{1,0:T(8,128)(2,1)S(1)}, bf16[512,1024]{1,0:T(8,128)(2,1)}, u32[]{:S(2)}) copy-start(bf16[512,1024]{1,0:T(8,128)(2,1)} %q_ref.7) | copy-start | bytes 3145732
  14.7 4.2 %collective-permute-start = (bf16[1024,128]{1,0:T(8,128)(2,1)S(1)}, bf16[1024,128]{1,0:T(8,128)(2,1)S(1)}, u32[]{:S(2)}, u32[]{:S(2)}) collective-permute-start(bf16[1024,128]{1,0:T(8,128)(2,1)S(1)} %get-tuple-element.16), channel_id=1, source_target_pairs={{0,4},{4,0},{8,12},{12,8},{16,20},{20,16},{24,28},{28,24},{32,36},... | collective-permute-start | bytes 786440 | tf_op jit(solution)/shard_map/ppermute | solution.py:283
  14.8 4.2 %collective-permute-start.2 = (bf16[1024,128]{1,0:T(8,128)(2,1)S(1)}, bf16[1024,128]{1,0:T(8,128)(2,1)S(1)}, u32[]{:S(2)}, u32[]{:S(2)}) collective-permute-start(bf16[1024,128]{1,0:T(8,128)(2,1)S(1)} %once_here.4.k2_ref), channel_id=1, source_target_pairs={{0,4},{4,0},{8,12},{12,8},{16,20},{20,16},{24,28},{28,24},{32,36},... | collective-permute-start | bytes 786440 | tf_op jit(solution)/shard_map/ppermute | solution.py:283
  19.0 7.4 %copy-start.1 = (bf16[512,1024]{1,0:T(8,128)(2,1)S(1)}, bf16[512,1024]{1,0:T(8,128)(2,1)}, u32[]{:S(2)}) copy-start(bf16[512,1024]{1,0:T(8,128)(2,1)} %q_ref.7) | copy-start | bytes 3145732
  22.5 19.2 %collective-permute-start.4 = (bf16[512,640]{1,0:T(8,128)(2,1)S(1)}, bf16[512,640]{1,0:T(8,128)(2,1)S(1)}, u32[]{:S(2)}, u32[]{:S(2)}) collective-permute-start(bf16[512,640]{1,0:T(8,128)(2,1)S(1)} %get-tuple-element.22.refs_0_), channel_id=1, source_target_pairs={{0,1},{1,2},{2,3},{3,0},{4,5},{5,6},{6,7},{7,4},{8,9},{9,10},{10,1... | collective-permute-start | bytes 1966088 | tf_op jit(solution)/shard_map/ppermute | solution.py:286
  24.2 17.5 %collective-permute-start.8 = (bf16[512,640]{1,0:T(8,128)(2,1)S(1)}, bf16[512,640]{1,0:T(8,128)(2,1)S(1)}, u32[]{:S(2)}, u32[]{:S(2)}) collective-permute-start(bf16[512,640]{1,0:T(8,128)(2,1)S(1)} %get-tuple-element.22.refs_0_), channel_id=1, source_target_pairs={{0,3},{1,0},{2,1},{3,2},{4,7},{5,4},{6,5},{7,6},{8,11},{9,8},{10,9... | collective-permute-start | bytes 1966088 | tf_op jit(solution)/shard_map/ppermute | solution.py:286
  32.8 15.7 %collective-permute-start.6 = (bf16[512,384]{1,0:T(8,128)(2,1)S(1)}, bf16[512,384]{1,0:T(8,128)(2,1)S(1)}, u32[]{:S(2)}, u32[]{:S(2)}) collective-permute-start(bf16[512,384]{1,0:T(8,128)(2,1)S(1)} %get-tuple-element.25.refs_1_), channel_id=1, source_target_pairs={{0,3},{1,0},{2,1},{3,2},{4,7},{5,4},{6,5},{7,6},{8,11},{9,8},{10,9... | collective-permute-start | bytes 1179656 | tf_op jit(solution)/shard_map/ppermute | solution.py:286
  34.3 15.8 %collective-permute-start.7 = (bf16[512,384]{1,0:T(8,128)(2,1)S(1)}, bf16[512,384]{1,0:T(8,128)(2,1)S(1)}, u32[]{:S(2)}, u32[]{:S(2)}) collective-permute-start(bf16[512,384]{1,0:T(8,128)(2,1)S(1)} %get-tuple-element.25.refs_1_), channel_id=1, source_target_pairs={{0,1},{1,2},{2,3},{3,0},{4,5},{5,6},{6,7},{7,4},{8,9},{9,10},{10,1... | collective-permute-start | bytes 1179656 | tf_op jit(solution)/shard_map/ppermute | solution.py:286
  41.6 20.8 %collective-permute-start.5 = (bf16[512,640]{1,0:T(8,128)(2,1)S(1)}, bf16[512,640]{1,0:T(8,128)(2,1)S(1)}, u32[]{:S(2)}, u32[]{:S(2)}) collective-permute-start(bf16[512,640]{1,0:T(8,128)(2,1)S(1)} %once_here.6.refs_0_), channel_id=1, source_target_pairs={{0,1},{1,2},{2,3},{3,0},{4,5},{5,6},{6,7},{7,4},{8,9},{9,10},{10,1... | collective-permute-start | bytes 1966088 | tf_op jit(solution)/shard_map/ppermute | solution.py:286
  50.1 10.4 %collective-permute-start.9 = (bf16[512,384]{1,0:T(8,128)(2,1)S(1)}, bf16[512,384]{1,0:T(8,128)(2,1)S(1)}, u32[]{:S(2)}, u32[]{:S(2)}) collective-permute-start(bf16[512,384]{1,0:T(8,128)(2,1)S(1)} %once_here.7.refs_1_), channel_id=1, source_target_pairs={{0,3},{1,0},{2,1},{3,2},{4,7},{5,4},{6,5},{7,6},{8,11},{9,8},{10,9... | collective-permute-start | bytes 1179656 | tf_op jit(solution)/shard_map/ppermute | solution.py:286
